TPU v7x, 256 devices: a whole 4x4x8 slice. The times are simulated.
256 devices in a mesh: section: 16 (over z_hi, x, core), tensor: 16 (over z_lo, y).
Axes of the slice: x: 4, y: 4, z: 8 (z_hi: 2, z_lo: 4; z = z_hi * 4 + z_lo), core: 2. Of those that a mesh axis runs over, the one named last changes fastest.
Arguments:
- entering: bfloat16 [2, 128, 4096], P(None, None, 'tensor'), may hold values from -6 to 6
- arriving: bfloat16 [16, 128, 4096], P('section', None, 'tensor'), may hold values from -6 to 6
- stashed: bfloat16 [16, 2, 128, 4096], P('section', None, None, 'tensor'), may hold values from -6 to 6
- parked: bfloat16 [16, 2, 128, 4096], P('section', None, None, 'tensor'), may hold values from -6 to 6
- evict: int32 [16, 2], P('section'), may hold values from 0 to 1, as said below
- cotangent: bfloat16 [2, 128, 4096], P(None, None, 'tensor'), may hold values from -6 to 6
- arriving_grad: bfloat16 [16, 128, 4096], P('section', None, 'tensor'), may hold values from -6 to 6
- qkv_weight: bfloat16 [16, 4096, 12288], P('section', None, 'tensor'), may hold values from -0.09375 to 0.09375
- out_weight: bfloat16 [16, 4096, 4096], P('section', 'tensor'), may hold values from -0.375 to 0.375
- norm_gain: float32 [16, 4096], P('section'), may hold values from 0.5 to 1.5
Outputs:
- section_outputs: bfloat16 [16, 2, 128, 4096], P('section', None, None, 'tensor')
- input_grads: bfloat16 [16, 2, 128, 4096], P('section', None, None, 'tensor')
- new_parked: bfloat16 [16, 2, 128, 4096], P('section', None, None, 'tensor')
Inputs may be any that keep to these rules, and one draw needn't show every extreme that they name: evict[15 - s, t] and evict[s, t] may both be 1; evict[0, 0] is 1 and evict[15, 1] is 0.
All inputs are finite; a program needn't handle non-finite values.
Results may differ from a plain program's by a relative error of at most 0.035.
Values may be sent and summed in bfloat16 or wider, within the bound.
A program may use at most 64 MiB of HBM per device.

v0:
```python
import math

import jax
import jax.numpy as jnp
from jax import lax
from jax.sharding import PartitionSpec as P

HEAD_DIM = 128


def partner(value, axis, distance):
    mask = 2**distance
    pairs = [(source, source ^ mask) for source in range(lax.axis_size(axis))]
    return lax.ppermute(value, axis, pairs)


def from_behind(block, axis, distance):
    devices = range(lax.axis_size(axis))
    route = [(i - distance, i) for i in devices if i - distance in devices]
    return lax.ppermute(block, axis, route)


def normalize(inflow):
    values = inflow.astype(jnp.float32)
    centre = jnp.mean(values, axis=-1, keepdims=True)
    shifted = values - centre
    spread = jnp.mean(shifted * shifted, axis=-1, keepdims=True)
    inv_scale = lax.rsqrt(spread + 1e-05)
    return (shifted * inv_scale, inv_scale)


def attend(projected, head_dim):
    tokens = projected.shape[0]
    parts = projected.astype(jnp.bfloat16).reshape(tokens, -1, 3, head_dim)
    queries = parts[:, :, 0, :]
    key_rows = parts[:, :, 1, :]
    value_rows = parts[:, :, 2, :]
    score_scale = 1.0 / math.sqrt(head_dim)
    scores = (
        jnp.einsum("qhd,khd->hqk", queries, key_rows, preferred_element_type=jnp.float32)
        * score_scale
    )
    later = lax.broadcasted_iota(jnp.int32, (tokens, tokens), 0)
    earlier = lax.broadcasted_iota(jnp.int32, (tokens, tokens), 1)
    exponent = jnp.where(earlier <= later, jnp.exp(scores), 0.0)
    probabilities = exponent / jnp.sum(exponent, axis=-1, keepdims=True)
    attn_weights = probabilities.astype(jnp.bfloat16)
    attended = jnp.einsum(
        "hqk,khd->qhd", attn_weights, value_rows, preferred_element_type=jnp.float32
    ).astype(jnp.bfloat16)
    return (queries, key_rows, value_rows, probabilities, attn_weights, attended)


def attend_back(
    queries, key_rows, value_rows, probabilities, attn_weights, grad_attended, head_dim
):
    tokens = queries.shape[0]
    score_scale = 1.0 / math.sqrt(head_dim)
    grad_values = jnp.einsum(
        "hqk,qhd->khd", attn_weights, grad_attended, preferred_element_type=jnp.float32
    ).astype(jnp.bfloat16)
    grad_probs = jnp.einsum(
        "qhd,khd->hqk", grad_attended, value_rows, preferred_element_type=jnp.float32
    )
    row_dot = jnp.sum(probabilities * grad_probs, axis=-1, keepdims=True)
    grad_scores = (probabilities * (grad_probs - row_dot) * score_scale).astype(jnp.bfloat16)
    grad_queries = jnp.einsum(
        "hqk,khd->qhd", grad_scores, key_rows, preferred_element_type=jnp.float32
    ).astype(jnp.bfloat16)
    grad_keys = jnp.einsum(
        "hqk,qhd->khd", grad_scores, queries, preferred_element_type=jnp.float32
    ).astype(jnp.bfloat16)
    return jnp.stack([grad_queries, grad_keys, grad_values], axis=2).reshape(tokens, -1)


def norm_backward(grad_normed, standard, inv_scale, scale_gain, upstream):
    grad_hat = grad_normed * scale_gain
    grad_local = inv_scale * (
        grad_hat
        - jnp.mean(grad_hat, axis=-1, keepdims=True)
        - standard * jnp.mean(grad_hat * standard, axis=-1, keepdims=True)
    )
    return (upstream.astype(jnp.float32) + grad_local).astype(jnp.bfloat16)


def on_device(
    entering,
    arriving,
    stashed,
    parked,
    evict,
    cotangent,
    arriving_grad,
    qkv_weight,
    out_weight,
    norm_gain,
):
    sections = lax.axis_size("section")
    section_index = lax.axis_index("section")
    window = entering.shape[0]
    seq_len = entering.shape[1]
    col_count = entering.shape[2]
    col_start = lax.axis_index("tensor") * col_count
    weight_in = qkv_weight[0]
    weight_out = out_weight[0]
    scale_gain = norm_gain[0]
    flags = evict[0]
    bit_count = sections.bit_length() - 1
    bit_order = list(range(bit_count))
    fetched = parked[0]
    for bit in bit_order:
        fetched = partner(fetched, "section", bit)
    chosen = jnp.where(flags[:, None, None] == 1, fetched, stashed[0])
    full_enter, full_stash, full_cot, full_arrive, full_arrive_grad = (
        lax.all_gather(entering, "tensor", axis=2, tiled=True),
        lax.all_gather(chosen, "tensor", axis=2, tiled=True),
        lax.all_gather(cotangent, "tensor", axis=2, tiled=True),
        lax.all_gather(arriving, "tensor", axis=2, tiled=True),
        lax.all_gather(arriving_grad, "tensor", axis=2, tiled=True),
    )
    produced_all = []
    inflow_cols = []
    current = full_arrive[0]
    for window_step in range(window):
        inflow = jnp.where(section_index == 0, full_enter[window_step], current)
        inflow_cols.append(lax.dynamic_slice_in_dim(inflow, col_start, col_count, 1))
        standard, inv_scale = normalize(inflow)
        normed = (standard * scale_gain).astype(jnp.bfloat16)
        projected = jnp.dot(normed, weight_in, preferred_element_type=jnp.float32)
        attended_flat = attend(projected, HEAD_DIM)[5].reshape(seq_len, -1)
        more_steps = window_step + 1 < window
        summed = lax.psum(
            jnp.dot(attended_flat, weight_out, preferred_element_type=jnp.float32).astype(
                jnp.bfloat16
            ),
            "tensor",
        ).astype(jnp.float32)
        produced = (inflow.astype(jnp.float32) + summed).astype(jnp.bfloat16)
        produced_all.append(lax.dynamic_slice_in_dim(produced, col_start, col_count, 1))
        if more_steps:
            current = from_behind(produced, "section", 1)
    inflow_stack = jnp.stack(inflow_cols)
    leaving = jnp.where(flags[:, None, None] == 1, inflow_stack, jnp.zeros_like(inflow_stack))
    for bit in bit_order:
        leaving = partner(leaving, "section", bit)
    passed_all = []
    current_grad = full_arrive_grad[0]
    for window_step in range(window):
        upstream = jnp.where(section_index == sections - 1, full_cot[window_step], current_grad)
        standard, inv_scale = normalize(full_stash[window_step])
        normed = (standard * scale_gain).astype(jnp.bfloat16)
        projected = jnp.dot(normed, weight_in, preferred_element_type=jnp.float32)
        queries, key_rows, value_rows, probabilities, attn_weights, attended = attend(
            projected, HEAD_DIM
        )
        grad_attended = (
            jnp.dot(upstream, weight_out.T, preferred_element_type=jnp.float32)
            .astype(jnp.bfloat16)
            .reshape(seq_len, -1, HEAD_DIM)
        )
        grad_projected = attend_back(
            queries, key_rows, value_rows, probabilities, attn_weights, grad_attended, HEAD_DIM
        )
        more_steps = window_step + 1 < window
        grad_normed = lax.psum(
            jnp.dot(grad_projected, weight_in.T, preferred_element_type=jnp.float32).astype(
                jnp.bfloat16
            ),
            "tensor",
        ).astype(jnp.float32)
        passed = norm_backward(grad_normed, standard, inv_scale, scale_gain, upstream)
        passed_all.append(lax.dynamic_slice_in_dim(passed, col_start, col_count, 1))
        if more_steps:
            current_grad = from_behind(passed, "section", -1)
    return (jnp.stack(produced_all)[None], jnp.stack(passed_all)[None], leaving[None])


def solution(mesh):
    in_specs = (
        P(None, None, "tensor"),
        P("section", None, "tensor"),
        P("section", None, None, "tensor"),
        P("section", None, None, "tensor"),
        P("section", None),
        P(None, None, "tensor"),
        P("section", None, "tensor"),
        P("section", None, "tensor"),
        P("section", "tensor", None),
        P("section", None),
    )
    out_specs = (
        P("section", None, None, "tensor"),
        P("section", None, None, "tensor"),
        P("section", None, None, "tensor"),
    )
    return jax.shard_map(
        on_device, mesh=mesh, in_specs=in_specs, out_specs=out_specs, check_vma=False
    )
```

profile of v0, /device:TPU:2, one launch (start us, length us, event | category | flops | bytes accessed | tf_op | source)
XLA Modules:
  0.0 803.8 jit_solution(2830513657582136021)
XLA Ops:
  10.1 1.5 collective-permute-done.1
  11.7 2.3 collective-permute-start.2
  13.9 3.8 collective-permute-done.2
  17.7 1.6 collective-permute-start.3
  19.3 4.9 collective-permute-done.3
  24.3 6.6 collective-permute-start.4
  31.5 4.3 collective-permute-done.4
  35.9 1.6 bitcast_select_fusion
  37.6 44.0 %all-gather.12.cloned.1.call-done = bf16[1,128,4096]{2,1,0:T(8,128)(2,1)} async-done(((bf16[1,128,256]{2,1,0:T(8,128)(2,1)}), bf16[1,128,4096]{2,1,0:T(8,128)(2,1)}) %all-gather.12.cloned.1.call-update) | async-done | bytes 1048592 | tf_op jit(solution)/shard_map/all_gather | solution.py:119
  81.6 75.2 %all-gather.10.cloned.1.call-done = bf16[2,128,4096]{2,1,0:T(8,128)(2,1)} async-done(((bf16[2,128,256]{2,1,0:T(8,128)(2,1)}), bf16[2,128,4096]{2,1,0:T(8,128)(2,1)}) %all-gather.10.cloned.1.call-update) | async-done | bytes 2097168 | tf_op jit(solution)/shard_map/all_gather | solution.py:117
  156.8 2.4 fusion.82
  159.3 66.7 %all-gather.8.cloned.1.call-done = bf16[1,128,4096]{2,1,0:T(8,128)(2,1)} async-done(((bf16[1,128,256]{2,1,0:T(8,128)(2,1)}), bf16[1,128,4096]{2,1,0:T(8,128)(2,1)}) %all-gather.8.cloned.1.call-update) | async-done | bytes 1048592 | tf_op jit(solution)/shard_map/all_gather | solution.py:118
  226.0 74.8 %all-gather.6.cloned.1.call-done = bf16[2,128,4096]{2,1,0:T(8,128)(2,1)} async-done(((bf16[2,128,256]{2,1,0:T(8,128)(2,1)}), bf16[2,128,4096]{2,1,0:T(8,128)(2,1)}) %all-gather.6.cloned.1.call-update) | async-done | bytes 2097168 | tf_op jit(solution)/shard_map/all_gather | solution.py:115
  300.8 2.0 convert_reduce_fusion.2
  303.3 3.8 fusion.56
  307.9 1.1 fusion.74
  309.0 1.0 convolution_convert_fusion.9
  310.1 1.5 convolution_convert_fusion.1
  311.5 65.0 %all-gather.14.cloned.1.call-done = bf16[2,128,4096]{2,1,0:T(8,128)(2,1)} async-done(((bf16[2,128,256]{2,1,0:T(8,128)(2,1)}), bf16[2,128,4096]{2,1,0:T(8,128)(2,1)}) %all-gather.14.cloned.1.call-update) | async-done | bytes 2097168 | tf_op jit(solution)/shard_map/all_gather | solution.py:116
  376.5 2.6 convert_reduce_fusion.1
  379.5 4.6 fusion.62
  384.1 1.1 copy.51
  385.2 0.9 fusion.143
  386.1 0.9 fusion.137
  387.0 1.1 fusion.92
  388.1 1.3 fusion.90
  389.3 1.3 fusion.91
  390.7 6.0 fusion.14
  397.3 167.1 %all-reduce.7.cloned.1.call-done = (bf16[128,4096]{1,0:T(8,128)(2,1)}, bf16[128,4096]{1,0:T(8,128)(2,1)}) async-done(((bf16[128,4096]{1,0:T(8,128)(2,1)}, bf16[128,4096]{1,0:T(8,128)(2,1)}), (bf16[128,4096]{1,0:T(8,128)(2,1)}, bf16[128,4096]{1,0:T(8,128)(2,1)})) %all-reduce.7.cloned.1.call-update) | async-done | bytes 2097168 | tf_op jit(solution)/shard_map/psum | solution.py:132
  564.4 3.0 fusion.33
  567.5 4.6 fusion.65
  572.1 1.1 copy.63
  573.2 4.4 fusion.37
  577.5 2.0 collective-permute-start.5
  579.6 1.3 fusion.24
  580.9 2.4 collective-permute-start
  583.3 0.9 fusion.140
  584.2 8.0 collective-permute-done.5
  592.2 1.7 fusion.102
  593.9 1.0 copy-done.4
  594.8 0.8 fusion.85
  596.0 1.8 fusion.93
  597.8 1.8 fusion.94
  599.6 1.2 fusion.95
  600.8 1.0 pad_maximum_fusion.1
  601.9 6.2 fusion.17
  608.1 1.6 convert_reduce_fusion.3
  610.7 1.1 fusion.59
  612.0 0.9 fusion.75
  613.2 1.4 convolution_convert_fusion
  614.7 0.9 dynamic-slice_bitcast_fusion
  615.6 2.1 collective-permute-start.6
  617.8 1.0 collective-permute-done.6
  619.0 5.5 collective-permute-done.7
  624.5 4.7 collective-permute-start.8
  629.2 3.2 collective-permute-done.8
  632.4 2.9 collective-permute-start.9
  635.3 0.8 dynamic-slice_bitcast_fusion.1
  636.1 0.8 dynamic-slice_bitcast_fusion.2
  637.0 2.7 convert_element_type.187
  639.7 3.4 collective-permute-done.9
  643.1 148.6 %all-reduce.5.cloned.1.call-done = (bf16[128,4096]{1,0:T(8,128)(2,1)}, bf16[128,4096]{1,0:T(8,128)(2,1)}) async-done(((bf16[128,4096]{1,0:T(8,128)(2,1)}, bf16[128,4096]{1,0:T(8,128)(2,1)}), (bf16[128,4096]{1,0:T(8,128)(2,1)}, bf16[128,4096]{1,0:T(8,128)(2,1)})) %all-reduce.5.cloned.1.call-update) | async-done | bytes 2097168 | tf_op jit(solution)/shard_map/psum | solution.py:132
  791.7 2.2 fusion.117
  793.9 1.1 fusion.134
  (94 shorter events, 10.2 us)
Async XLA Ops:
  7.2 149.7 %copy-start = (bf16[1,256,4096]{2,1,0:T(8,128)(2,1)S(1)}, bf16[1,256,4096]{2,1,0:T(8,128)(2,1)}, u32[]{:S(2)}) copy-start(bf16[1,256,4096]{2,1,0:T(8,128)(2,1)} %param.18) | copy-start | bytes 6291460
  7.2 74.4 %all-gather.12.cloned.1.call-start = ((), (), s32[]{:S(2)}) async-start(), calls=%async_computation.3 | async-start | bytes 1114112 | tf_op jit(solution)/shard_map/all_gather | solution.py:119
  7.9 148.9 %all-gather.10.cloned.1.call-start = ((), (), s32[]{:S(2)}) async-start(), calls=%async_computation.2 | async-start | bytes 2228224 | tf_op jit(solution)/shard_map/all_gather | solution.py:117
  8.7 217.4 %all-gather.8.cloned.1.call-start = ((), (), s32[]{:S(2)}) async-start(), calls=%async_computation.1 | async-start | bytes 1114112 | tf_op jit(solution)/shard_map/all_gather | solution.py:118
  9.4 291.4 %all-gather.6.cloned.1.call-start = ((), (), s32[]{:S(2)}) async-start(), calls=%async_computation | async-start | bytes 2228224 | tf_op jit(solution)/shard_map/all_gather | solution.py:115
  10.0 366.5 %all-gather.14.cloned.1.call-start = ((), (), s32[]{:S(2)}) async-start(), calls=%async_computation.4 | async-start | bytes 2228224 | tf_op jit(solution)/shard_map/all_gather | solution.py:116
  10.0 1.6 collective-permute-start.1
  11.7 6.1 collective-permute-start.2
  17.7 6.5 collective-permute-start.3
  24.3 11.6 %collective-permute-start.4 = (bf16[2,128,256]{2,1,0:T(8,128)(2,1)S(1)}, bf16[2,128,256]{2,1,0:T(8,128)(2,1)S(1)}, u32[]{:S(2)}, u32[]{:S(2)}) collective-permute-start(bf16[2,128,256]{2,1,0:T(8,128)(2,1)S(1)} %collective-permute-done.3), channel_id=1, source_target_pairs={{0,128},{16,144},{32,160},{48,176},{64,192},{80,208},{96,224},{112... | collective-permute-start | bytes 393224 | tf_op jit(solution)/shard_map/ppermute | solution.py:14
  31.5 4.3 copy-start.12
  37.5 526.9 %all-reduce.7.cloned.1.call-start = ((), (), s32[]{:S(2)}) async-start(), calls=%async_computation.6 | async-start | bytes 4194304 | tf_op jit(solution)/shard_map/psum | solution.py:132
  37.6 347.6 %copy-start.8 = (pred[128,128]{0,1:T(8,128)(4,1)}, pred[128,128]{0,1:T(8,128)(4,1)S(1)}, u32[]{:S(2)}) copy-start(pred[128,128]{0,1:T(8,128)(4,1)S(1)} %iota_compare_fusion) | copy-start | bytes 49156
  159.3 143.9 %copy-start.7 = (f32[1,4096]{1,0:T(1,128)S(1)}, f32[1,4096]{1,0:T(1,128)}, u32[]{:S(2)}) copy-start(f32[1,4096]{1,0:T(1,128)} %param.19) | copy-start | bytes 49156
  376.5 2.6 copy-start.1
  379.1 5.0 copy-start.10
  379.5 4.6 copy-start.18
  396.7 0.7 copy-start.20
  396.7 167.8 %copy-start.11 = (f32[128]{0:T(128)S(1)}, f32[128]{0:T(128)}, u32[]{:S(2)}) copy-start(f32[128]{0:T(128)} %copy-done.10) | copy-start | bytes 1540
  396.7 167.8 %copy-start.19 = (f32[128]{0:T(128)S(1)}, f32[128]{0:T(128)}, u32[]{:S(2)}) copy-start(f32[128]{0:T(128)} %copy-done.18) | copy-start | bytes 1540
  396.7 395.0 %all-reduce.5.cloned.1.call-start = ((), (), s32[]{:S(2)}) async-start(), calls=%async_computation.5 | async-start | bytes 4194304 | tf_op jit(solution)/shard_map/psum | solution.py:132
  397.3 174.7 %copy-start.14 = (f32[128]{0:T(128)}, f32[128]{0:T(128)S(1)}, u32[]{:S(2)}) copy-start(f32[128]{0:T(128)S(1)} %broadcast_multiply_fusion.2) | copy-start | bytes 1540
  564.4 3.0 copy-start.2
  567.5 4.6 copy-start.16
  573.2 6.4 copy-start.6
  577.5 5.7 copy-start.9
  577.5 14.7 %collective-permute-start.5 = (bf16[128,4096]{1,0:T(8,128)(2,1)}, bf16[128,4096]{1,0:T(8,128)(2,1)}, u32[]{:S(2)}, u32[]{:S(2)}) collective-permute-start(bf16[128,4096]{1,0:T(8,128)(2,1)} %fusion.37), channel_id=1, source_target_pairs={{16,0},{32,16},{48,32},{64,48},{80,64},{96,80},{112,96},{128,112},... | collective-permute-start | bytes 3145736 | tf_op jit(solution)/shard_map/ppermute | solution.py:20
  580.9 27.3 %collective-permute-start = (bf16[128,4096]{1,0:T(8,128)(2,1)}, bf16[128,4096]{1,0:T(8,128)(2,1)}, u32[]{:S(2)}, u32[]{:S(2)}) collective-permute-start(bf16[128,4096]{1,0:T(8,128)(2,1)} %fusion.24), channel_id=1, source_target_pairs={{0,16},{16,32},{32,48},{48,64},{64,80},{80,96},{96,112},{112,128},... | collective-permute-start | bytes 3145736 | tf_op jit(solution)/shard_map/ppermute | solution.py:20
  593.9 1.0 copy-start.4
  599.6 11.1 %slice-start = ((s8[6291456]{0:T(1024)(128)(4,1)}), s8[4194304]{0:T(1024)(128)(4,1)S(1)}, s32[]{:S(2)}) async-start(s8[6291456]{0:T(1024)(128)(4,1)} %bitcast.245), calls=%async_computation.7 | async-start | bytes 8388608
  601.9 6.2 copy-start.5
  601.9 8.9 %slice-start.1 = ((s8[6291456]{0:T(1024)(128)(4,1)}), s8[2097152]{0:T(1024)(128)(4,1)S(1)}, s32[]{:S(2)}) async-start(s8[6291456]{0:T(1024)(128)(4,1)} %bitcast.245), calls=%async_computation.8 | async-start | bytes 4194304
  609.7 1.0 copy-start.3
  613.2 2.4 copy-start.13
  614.6 177.1 %copy-start.15 = (f32[128]{0:T(128)S(1)}, f32[128]{0:T(128)}, u32[]{:S(2)}) copy-start(f32[128]{0:T(128)} %copy-done.14) | copy-start | bytes 1540
  614.6 177.1 %copy-start.17 = (f32[128]{0:T(128)S(1)}, f32[128]{0:T(128)}, u32[]{:S(2)}) copy-start(f32[128]{0:T(128)} %copy-done.16) | copy-start | bytes 1540
  615.6 3.1 collective-permute-start.6
  618.7 5.8 collective-permute-start.7
  624.5 7.9 collective-permute-start.8
  632.4 10.7 %collective-permute-start.9 = (bf16[2,128,256]{2,1,0:T(8,128)(2,1)S(1)}, bf16[2,128,256]{2,1,0:T(8,128)(2,1)S(1)}, u32[]{:S(2)}, u32[]{:S(2)}) collective-permute-start(bf16[2,128,256]{2,1,0:T(8,128)(2,1)S(1)} %collective-permute-done.8), channel_id=1, source_target_pairs={{0,128},{16,144},{32,160},{48,176},{64,192},{80,208},{96,224},{112... | collective-permute-start | bytes 393224 | tf_op jit(solution)/shard_map/ppermute | solution.py:14
Sparse Core Ops, SparseCore 0:
  9.7 71.8 all-gather.11
  83.3 73.4 all-gather.9
  158.6 67.4 all-gather.7
  227.6 73.1 all-gather.5
  303.0 73.4 all-gather.13
  396.8 167.5 all-reduce.6
  614.8 176.8 all-reduce.4
where the time goes:
time: 805 us; the launch traced here: 804 us
  waiting for transfers between devices  680 us (84%)
  matrix products  47.1 us (6%)
  other arithmetic  28.5 us (4%)
  starting transfers between devices  25.4 us (3%)
  between operations  14.5 us (2%)
  local copies, waits for them, and re-layouts  8.59 us (1%)
    psum x2, waiting for transfers between devices, on_device(): lax.psum(jnp.dot(attended_flat, weight_out, preferred_element_type=jnp.fl...  316 us
    all_gather x1, waiting for transfers between devices, on_device(): lax.all_gather(cotangent, 'tensor', axis=2, tiled=True)  75.2 us
    all_gather x1, waiting for transfers between devices, on_device(): lax.all_gather(entering, 'tensor', axis=2, tiled=True)  74.8 us
    all_gather x1, waiting for transfers between devices, on_device(): lax.all_gather(arriving, 'tensor', axis=2, tiled=True)  66.7 us
    all_gather x1, waiting for transfers between devices, on_device(): lax.all_gather(chosen, 'tensor', axis=2, tiled=True)  65 us
    all_gather x1, waiting for transfers between devices, on_device(): lax.all_gather(arriving_grad, 'tensor', axis=2, tiled=True)  44 us
    ppermute x8, waiting for transfers between devices, partner(): return lax.ppermute(value, axis, pairs)  27.7 us
    ppermute x8, starting transfers between devices, partner(): return lax.ppermute(value, axis, pairs)  20.5 us
  transfers between devices with their start and end apart: 17, of which 16 were waited for; matrix products, arithmetic and copies ran while one was open for 5% of the time, Pallas kernels for 0%

commit v1 on v0

v1 whole, which is shorter than its diff:
```python
import functools
import math

import jax
import jax.numpy as jnp
from jax import lax
from jax.experimental import pallas as pl
from jax.experimental.pallas import tpu as pltpu
from jax.sharding import PartitionSpec as P

MESH = pl.DeviceIdType.MESH
HD = 128
BF = jnp.bfloat16
F32 = jnp.float32

X0, U0, H0, H1, X1, U1 = range(6)
RF0, RB0, RF1, RB1 = range(4)


def dot(a, b):
    return lax.dot_general(a, b, (((1,), (0,)), ((), ())), preferred_element_type=F32)


def dot_nt(a, b):
    return lax.dot_general(a, b, (((1,), (1,)), ((), ())), preferred_element_type=F32)


def dot_tn(a, b):
    return lax.dot_general(a, b, (((0,), (0,)), ((), ())), preferred_element_type=F32)


def kernel(
    ent, arr, stash, park, flags, cot, agr, wq_h, wo_h, gain_h,
    out_f, out_b, out_p,
    wq, wo, gain, stv, prk, flv, ag, normed, proj, att, gab, gpb, wgs,
    pbuf, dbuf, zbuf, rrecv, drecv, zrecv, zown, sbuf, srecv, szbuf, szrecv, ostage, pstage,
    lsem, ag_s, agz_r, agy_r, rs_s, rsr_r, rsd_r, rsz_r, st_s, st_r, m_s, m_r, hop_s, hop_r, o_s,
):
    s, t = lax.axis_index("section"), lax.axis_index("tensor")
    sections = lax.axis_size("section")
    y, z = lax.rem(t, 4), lax.div(t, 4)
    yi = [y, lax.rem(y + 1, 4), lax.rem(y + 2, 4), lax.rem(y + 3, 4)]
    zi = [z, lax.rem(z + 1, 4), lax.rem(z + 2, 4), lax.rem(z + 3, 4)]
    nxt, prv = lax.rem(s + 1, sections), lax.rem(s + sections - 1, sections)
    mir = sections - 1 - s
    ydev = lambda j: (s, z * 4 + yi[j])
    zdev = lambda k: (s, zi[k] * 4 + y)
    feats = normed.shape[1]

    def chunk(yy, zz):
        return yy * 4 + zz

    def cols(yy, zz):
        return pl.ds(pl.multiple_of((zz * 4 + yy) * 256, 256), 256)

    own = chunk(y, z)
    my_cols = cols(y, z)

    def rcopy(src, dst, ss, rs, dev):
        return pltpu.make_async_remote_copy(
            src_ref=src, dst_ref=dst, send_sem=ss, recv_sem=rs, device_id=dev, device_id_type=MESH
        )

    @pl.when(s == 0)
    def _():
        pltpu.make_async_copy(ent.at[0], ag.at[X0, own], lsem.at[0]).start()

    @pl.when(s > 0)
    def _():
        pltpu.make_async_copy(arr.at[0], ag.at[X0, own], lsem.at[0]).start()

    @pl.when(s == sections - 1)
    def _():
        pltpu.make_async_copy(cot.at[0], ag.at[U0, own], lsem.at[1]).start()

    @pl.when(s < sections - 1)
    def _():
        pltpu.make_async_copy(agr.at[0], ag.at[U0, own], lsem.at[1]).start()

    load_stash = pltpu.make_async_copy(stash.at[0], stv, lsem.at[2])
    load_stash.start()
    load_flags = pltpu.make_async_copy(flags, flv, lsem.at[6])
    load_flags.start()
    load_gain = pltpu.make_async_copy(gain_h, gain, lsem.at[3])
    load_gain.start()
    load_wq = pltpu.make_async_copy(wq_h.at[0], wq, lsem.at[4])
    load_wq.start()
    load_wo = pltpu.make_async_copy(wo_h.at[0], wo, lsem.at[5])
    load_wo.start()

    barrier = pltpu.get_barrier_semaphore()
    peers = [ydev(1), ydev(2), ydev(3), zdev(1), zdev(2), zdev(3), (nxt, t), (prv, t), (mir, t)]
    for dev in peers:
        pl.semaphore_signal(barrier, inc=1, device_id=dev, device_id_type=MESH)
    pl.semaphore_wait(barrier, len(peers))

    def gz_copy(a, k):
        return rcopy(ag.at[a, own], ag.at[a, own], ag_s.at[a], agz_r.at[a, k - 1], zdev(k))

    def gz_wait(a, k):
        c = chunk(y, zi[(4 - k) % 4])
        rcopy(ag.at[a, c], ag.at[a, c], ag_s.at[a], agz_r.at[a, k - 1], zdev((4 - k) % 4)).wait_recv()

    def ag_z(a):
        for k in (1, 3, 2):
            gz_copy(a, k).start()

    def ag_y1(a, k):
        c = chunk(y, zi[(4 - k) % 4])
        if k:
            gz_wait(a, k)
        rcopy(ag.at[a, c], ag.at[a, c], ag_s.at[a], agy_r.at[a, 0, k], ydev(1)).start()
        rcopy(ag.at[a, c], ag.at[a, c], ag_s.at[a], agy_r.at[a, 1, k], ydev(3)).start()

    def ag_y2(a, k):
        zz = zi[(4 - k) % 4]
        c = chunk(yi[3], zz)
        rcopy(ag.at[a, c], ag.at[a, c], ag_s.at[a], agy_r.at[a, 0, k], ydev(3)).wait_recv()
        top = ag.at[a, c, pl.ds(0, 64)]
        rcopy(top, top, ag_s.at[a], agy_r.at[a, 2, k], ydev(1)).start()
        c = chunk(yi[1], zz)
        rcopy(ag.at[a, c], ag.at[a, c], ag_s.at[a], agy_r.at[a, 1, k], ydev(1)).wait_recv()
        low = ag.at[a, c, pl.ds(64, 64)]
        rcopy(low, low, ag_s.at[a], agy_r.at[a, 3, k], ydev(3)).start()

    def ag_fin(a):
        for k in (0, 1, 3, 2):
            c = chunk(yi[2], zi[(4 - k) % 4])
            top, low = ag.at[a, c, pl.ds(0, 64)], ag.at[a, c, pl.ds(64, 64)]
            rcopy(top, top, ag_s.at[a], agy_r.at[a, 2, k], ydev(3)).wait_recv()
            rcopy(low, low, ag_s.at[a], agy_r.at[a, 3, k], ydev(1)).wait_recv()

    def y1_rest(a):
        for k in (1, 3, 2):
            ag_y1(a, k)

    def y2_all(a):
        for k in (0, 1, 3, 2):
            ag_y2(a, k)

    def layer_norm(a):
        def add(c, acc):
            return acc + ag[a, c].astype(F32)

        acc = lax.fori_loop(0, 16, add, jnp.zeros((128, 256), F32))
        mean = jnp.sum(acc, axis=1, keepdims=True) * (1.0 / feats)

        def var(c, acc):
            d = ag[a, c].astype(F32) - mean
            return acc + d * d

        acc = lax.fori_loop(0, 16, var, jnp.zeros((128, 256), F32))
        inv = lax.rsqrt(jnp.sum(acc, axis=1, keepdims=True) * (1.0 / feats) + 1e-05)

        def put(c, carry):
            cc = cols(lax.div(c, 4), lax.rem(c, 4))
            normed[:, cc] = ((ag[a, c].astype(F32) - mean) * inv * gain[:, cc]).astype(BF)
            return carry

        lax.fori_loop(0, 16, put, 0)
        return mean, inv

    def qkv():
        def tile(n, carry):
            nn = pl.ds(pl.multiple_of(n * 256, 256), 256)
            proj[:, nn] = dot(normed[...], wq[:, nn])
            return carry

        lax.fori_loop(0, 3, tile, 0)

    scale = 1.0 / math.sqrt(HD)

    def attention():
        rows = lax.broadcasted_iota(jnp.int32, (128, 128), 0)
        lanes = lax.broadcasted_iota(jnp.int32, (128, 128), 1)
        out = []
        for h in range(2):
            q, k, v = (proj[:, h * 384 + i * 128 : h * 384 + (i + 1) * 128].astype(BF) for i in range(3))
            e = jnp.where(lanes <= rows, jnp.exp(dot_nt(q, k) * scale), 0.0)
            p = e / jnp.sum(e, axis=1, keepdims=True)
            out.append((q, k, v, p, p.astype(BF)))
        return out

    def attended(heads):
        for h, (q, k, v, p, w) in enumerate(heads):
            att[:, h * 128 : (h + 1) * 128] = dot(w, v).astype(BF)

    def grad_att(a):
        def step(c, acc):
            return acc + dot_nt(ag[a, c], wo[:, cols(lax.div(c, 4), lax.rem(c, 4))])

        gab[...] = lax.fori_loop(0, 16, step, jnp.zeros((128, 256), F32)).astype(BF)

    def attend_back(heads):
        for h, (q, k, v, p, w) in enumerate(heads):
            ga = gab[:, h * 128 : (h + 1) * 128]
            gv = dot_tn(w, ga).astype(BF)
            g = dot_nt(ga, v)
            gs = (p * (g - jnp.sum(p * g, axis=1, keepdims=True)) * scale).astype(BF)
            gpb[:, h * 384 : h * 384 + 128] = dot(gs, k).astype(BF)
            gpb[:, h * 384 + 128 : h * 384 + 256] = dot_tn(gs, q).astype(BF)
            gpb[:, h * 384 + 256 : h * 384 + 384] = gv

    def stats_start(tick):
        g = gpb[...].astype(F32)
        s1 = jnp.sum(g * wgs[...], axis=1, keepdims=True)
        s2 = jnp.sum(g * proj[...], axis=1, keepdims=True)
        lanes = lax.broadcasted_iota(jnp.int32, (128, 128), 1)
        both = jnp.where(lanes == 0, s1, jnp.where(lanes == 1, s2, 0.0))
        sbuf[tick] = both.T[0:8]
        for j in (1, 2, 3):
            rcopy(sbuf.at[tick], srecv.at[tick, j - 1], st_s.at[tick, j - 1], st_r.at[tick, j - 1], ydev(j)).start()

    def stats_mid(tick):
        for j in (1, 2, 3):
            rcopy(sbuf.at[tick], srecv.at[tick, j - 1], st_s.at[tick, j - 1], st_r.at[tick, j - 1], ydev(4 - j)).wait()
        szbuf[tick] = sbuf[tick] + srecv[tick, 0] + srecv[tick, 1] + srecv[tick, 2]
        for k in (1, 2, 3):
            rcopy(szbuf.at[tick], szrecv.at[tick, k - 1], st_s.at[tick, k + 2], st_r.at[tick, k + 2], zdev(k)).start()

    def stats_end(tick):
        for k in (1, 2, 3):
            rcopy(szbuf.at[tick], szrecv.at[tick, k - 1], st_s.at[tick, k + 2], st_r.at[tick, k + 2], zdev(4 - k)).wait()
        total = szbuf[tick] + szrecv[tick, 0] + szrecv[tick, 1] + szrecv[tick, 2]
        back = jnp.concatenate([total, jnp.zeros((120, 128), F32)], axis=0).T
        return back[:, 0:1] * (1.0 / feats), back[:, 1:2] * (1.0 / feats)

    KS = (1, 3, 2, 0)

    def part(r, yy, zz):
        if r in (RF0, RF1):
            return dot(att[...], wo[:, cols(yy, zz)])
        return dot_nt(gpb[...], wq[cols(yy, zz), :])

    def rs_o(r):
        for k in KS:
            pbuf[r, 2, k] = part(r, yi[2], zi[k]).astype(BF)
            top, low = pl.ds(0, 64), pl.ds(64, 64)
            rcopy(pbuf.at[r, 2, k, top], rrecv.at[r, k, top], rs_s.at[r], rsr_r.at[r, 0, k], ydev(1)).start()
            rcopy(pbuf.at[r, 2, k, low], rrecv.at[r, k, low], rs_s.at[r], rsr_r.at[r, 1, k], ydev(3)).start()
        for k in KS:
            pbuf[r, 1, k] = part(r, yi[1], zi[k]).astype(BF)
            pbuf[r, 3, k] = part(r, yi[3], zi[k]).astype(BF)
        for k in KS:
            pbuf[r, 0, k] = part(r, y, zi[k]).astype(BF)

    def rs_d(r):
        top, low = pl.ds(0, 64), pl.ds(64, 64)
        for k in KS:
            rcopy(pbuf.at[r, 2, k, top], rrecv.at[r, k, top], rs_s.at[r], rsr_r.at[r, 0, k], ydev(3)).wait_recv()
            dbuf[r, 0, k, 0:64] = (pbuf[r, 1, k, 0:64].astype(F32) + rrecv[r, k, 0:64].astype(F32)).astype(BF)
            dbuf[r, 0, k, 64:128] = pbuf[r, 1, k, 64:128]
            rcopy(dbuf.at[r, 0, k], drecv.at[r, 0, k], rs_s.at[r], rsd_r.at[r, 0, k], ydev(1)).start()
            rcopy(pbuf.at[r, 2, k, low], rrecv.at[r, k, low], rs_s.at[r], rsr_r.at[r, 1, k], ydev(1)).wait_recv()
            dbuf[r, 1, k, 0:64] = pbuf[r, 3, k, 0:64]
            dbuf[r, 1, k, 64:128] = (pbuf[r, 3, k, 64:128].astype(F32) + rrecv[r, k, 64:128].astype(F32)).astype(BF)
            rcopy(dbuf.at[r, 1, k], drecv.at[r, 1, k], rs_s.at[r], rsd_r.at[r, 1, k], ydev(3)).start()

    def rs_z(r):
        for k in KS:
            rcopy(dbuf.at[r, 0, k], drecv.at[r, 0, k], rs_s.at[r], rsd_r.at[r, 0, k], ydev(3)).wait_recv()
            rcopy(dbuf.at[r, 1, k], drecv.at[r, 1, k], rs_s.at[r], rsd_r.at[r, 1, k], ydev(1)).wait_recv()
            total = pbuf[r, 0, k].astype(F32) + drecv[r, 0, k].astype(F32) + drecv[r, 1, k].astype(F32)
            if k:
                zbuf[r, k - 1] = total.astype(BF)
                rcopy(zbuf.at[r, k - 1], zrecv.at[r, k - 1], rs_s.at[r], rsz_r.at[r, k - 1], zdev(k)).start()
            else:
                zown[r] = total

    def rs_fin(r):
        for k in (1, 3, 2):
            rcopy(zbuf.at[r, k - 1], zrecv.at[r, k - 1], rs_s.at[r], rsz_r.at[r, k - 1], zdev(4 - k)).wait_recv()
        return (
            zown[r] + zrecv[r, 0].astype(F32) + zrecv[r, 1].astype(F32) + zrecv[r, 2].astype(F32)
        )

    def forward_end(tick):
        total = rs_fin(RF1 if tick else RF0)
        ostage[tick] = (ag[X1 if tick else X0, own].astype(F32) + total).astype(BF)
        pltpu.make_async_copy(ostage.at[tick], out_f.at[0, tick], o_s.at[tick]).start()

    def backward_end(tick, mean, inv):
        total = rs_fin(RB1 if tick else RB0)
        m1, m2 = stats_end(tick)
        std = (ag[H1 if tick else H0, own].astype(F32) - mean) * inv
        grad = inv * (total * gain[:, my_cols] - m1 - std * m2)
        ostage[2 + tick] = (ag[U1 if tick else U0, own].astype(F32) + grad).astype(BF)
        pltpu.make_async_copy(ostage.at[2 + tick], out_b.at[0, tick], o_s.at[2 + tick]).start()

    def hop_start(slot, a, forward):
        cp = rcopy(ostage.at[slot], ag.at[a, own], hop_s.at[slot // 2], hop_r.at[slot // 2], (nxt if forward else prv, t))

        @pl.when((s < sections - 1) if forward else (s > 0))
        def _():
            cp.start()

    def hop_wait(slot, a, forward, first):
        cp = rcopy(ostage.at[slot], ag.at[a, own], hop_s.at[slot // 2], hop_r.at[slot // 2], (prv if forward else nxt, t))

        @pl.when((s > 0) if forward else (s < sections - 1))
        def _():
            cp.wait_recv()

        @pl.when((s == 0) if forward else (s == sections - 1))
        def _():
            own_copy = pltpu.make_async_copy(first, ag.at[a, own], lsem.at[slot // 2])
            own_copy.start()
            own_copy.wait()

    def mirror_copy(tick):
        return rcopy(park.at[0, tick], prk.at[tick], m_s.at[tick], m_r.at[tick], (mir, t))

    def parked_copy(tick):
        return rcopy(pstage.at[tick], out_p.at[0, tick], m_s.at[2 + tick], m_r.at[2 + tick], (mir, t))

    def park_inflow(tick):
        mine = ag[X1 if tick else X0, own]
        pstage[tick] = jnp.where(flv[tick] == 1, mine.astype(F32), 0.0).astype(BF)
        parked_copy(tick).start()

    def choose(tick):
        mirror_copy(tick).wait_recv()
        ag[H1 if tick else H0, own] = jnp.where(
            flv[tick] == 1, prk[tick].astype(F32), stv[tick].astype(F32)
        ).astype(BF)

    mirror_copy(0).start()
    pltpu.make_async_copy(arr.at[0], ag.at[X0, own], lsem.at[0]).wait()
    ag_z(X0)
    ag_y1(X0, 0)
    pltpu.make_async_copy(agr.at[0], ag.at[U0, own], lsem.at[1]).wait()
    mirror_copy(1).start()
    ag_z(U0)
    ag_y1(U0, 0)
    load_stash.wait()
    load_flags.wait()
    load_gain.wait()
    load_wq.wait()
    load_wo.wait()
    y1_rest(X0)
    y1_rest(U0)
    y2_all(X0)
    choose(0)
    ag_z(H0)
    ag_y1(H0, 0)
    g_hi = gain[...].astype(BF)
    g_lo = (gain[...] - g_hi.astype(F32)).astype(BF)
    sub = lax.broadcasted_iota(jnp.int32, (16, 128), 0)
    for c in range(feats // 128):
        hi, lo = g_hi[:, c * 128 : (c + 1) * 128].astype(F32), g_lo[:, c * 128 : (c + 1) * 128].astype(F32)
        normed[0:16, c * 128 : (c + 1) * 128] = jnp.where(sub == 0, hi, jnp.where(sub == 1, lo, 0.0)).astype(BF)

    def wg_tile(n, carry):
        nn = pl.ds(pl.multiple_of(n * 256, 256), 256)
        wgs[:, nn] = jnp.sum(dot(normed[0:16, :], wq[:, nn]), axis=0, keepdims=True)
        return carry

    lax.fori_loop(0, 3, wg_tile, 0)
    y2_all(U0)
    choose(1)
    y1_rest(H0)
    ag_fin(X0)
    layer_norm(X0)
    qkv()
    attended(attention())
    rs_o(RF0)
    y2_all(H0)
    ag_z(H1)
    rs_d(RF0)
    ag_fin(U0)
    grad_att(U0)
    park_inflow(0)
    rs_z(RF0)
    ag_fin(H0)
    mean0, inv0 = layer_norm(H0)
    qkv()
    heads = attention()
    attend_back(heads)
    stats_start(0)
    rs_o(RB0)
    forward_end(0)
    hop_start(0, X1, True)
    rs_d(RB0)
    ag_y1(H1, 0)
    y1_rest(H1)
    stats_mid(0)
    hop_wait(0, X1, True, ent.at[1])
    ag_z(X1)
    ag_y1(X1, 0)
    rs_z(RB0)
    y1_rest(X1)
    y2_all(H1)
    backward_end(0, mean0, inv0)
    hop_start(2, U1, False)
    y2_all(X1)
    ag_fin(H1)
    hop_wait(2, U1, False, cot.at[1])
    ag_z(U1)
    ag_y1(U1, 0)
    ag_fin(X1)
    layer_norm(X1)
    qkv()
    attended(attention())
    y1_rest(U1)
    rs_o(RF1)
    y2_all(U1)
    rs_d(RF1)
    mean1, inv1 = layer_norm(H1)
    qkv()
    heads = attention()
    park_inflow(1)
    rs_z(RF1)
    ag_fin(U1)
    grad_att(U1)
    attend_back(heads)
    stats_start(1)
    rs_o(RB1)
    rs_d(RB1)
    stats_mid(1)
    forward_end(1)
    rs_z(RB1)
    backward_end(1, mean1, inv1)

    for a in range(6):
        pltpu.make_async_copy(ag.at[a, pl.ds(0, 15)], ag.at[a, pl.ds(0, 15)], ag_s.at[a]).wait()
    for r in range(4):
        pltpu.make_async_copy(ag.at[0, pl.ds(0, 15)], ag.at[0, pl.ds(0, 15)], rs_s.at[r]).wait()
    for tick in range(2):
        mirror_copy(tick).wait_send()
        parked_copy(tick).wait()
        pltpu.make_async_copy(ostage.at[tick], out_f.at[0, tick], o_s.at[tick]).wait()
        pltpu.make_async_copy(ostage.at[2 + tick], out_b.at[0, tick], o_s.at[2 + tick]).wait()

    @pl.when(s < sections - 1)
    def _():
        rcopy(ostage.at[0], ag.at[X1, own], hop_s.at[0], hop_r.at[0], (nxt, t)).wait_send()

    @pl.when(s > 0)
    def _():
        rcopy(ostage.at[2], ag.at[U1, own], hop_s.at[1], hop_r.at[1], (prv, t)).wait_send()


def on_device(entering, arriving, stashed, parked, evict, cotangent, arriving_grad, qkv_weight, out_weight, norm_gain):
    any_spec = pl.BlockSpec(memory_space=pl.ANY)
    flags = jnp.broadcast_to(evict[0][:, None, None], (2, 128, 256))
    piece = lambda *lead: pltpu.VMEM(tuple(lead) + (128, 256), BF)
    dma = lambda *shape: pltpu.SemaphoreType.DMA(shape)
    slab = jax.ShapeDtypeStruct((1, 2, 128, 256), BF)
    return pl.pallas_call(
        kernel,
        out_shape=(slab, slab, slab),
        in_specs=[any_spec] * 10,
        out_specs=(any_spec,) * 3,
        scratch_shapes=[
            pltpu.VMEM(qkv_weight.shape[1:], BF),
            pltpu.VMEM(out_weight.shape[1:], BF),
            pltpu.VMEM(norm_gain.shape, F32),
            piece(2),
            piece(2),
            pltpu.VMEM((2, 128, 256), jnp.int32),
            piece(6, 16),
            pltpu.VMEM((128, 4096), BF),
            pltpu.VMEM((128, 768), F32),
            pltpu.VMEM((128, 256), BF),
            pltpu.VMEM((128, 256), BF),
            pltpu.VMEM((128, 768), BF),
            pltpu.VMEM((1, 768), F32),
            piece(4, 4, 4),
            piece(4, 2, 4),
            piece(4, 3),
            piece(4, 4),
            piece(4, 2, 4),
            piece(4, 3),
            pltpu.VMEM((4, 128, 256), F32),
            pltpu.VMEM((2, 8, 128), F32),
            pltpu.VMEM((2, 3, 8, 128), F32),
            pltpu.VMEM((2, 8, 128), F32),
            pltpu.VMEM((2, 3, 8, 128), F32),
            piece(4),
            piece(2),
            dma(7),
            dma(6),
            dma(6, 3),
            dma(6, 4, 4),
            dma(4),
            dma(4, 2, 4),
            dma(4, 2, 4),
            dma(4, 3),
            dma(2, 6),
            dma(2, 6),
            dma(4),
            dma(4),
            dma(2),
            dma(2),
            dma(4),
        ],
        compiler_params=pltpu.CompilerParams(
            collective_id=0, has_side_effects=True, vmem_limit_bytes=56 * 2**20
        ),
        cost_estimate=pl.CostEstimate(flops=6 * 10**9, bytes_accessed=10**7, transcendentals=10**5),
        name="relay_window",
    )(entering, arriving, stashed, parked, flags, cotangent, arriving_grad, qkv_weight, out_weight, norm_gain)


def solution(mesh):
    in_specs = (
        P(None, None, "tensor"),
        P("section", None, "tensor"),
        P("section", None, None, "tensor"),
        P("section", None, None, "tensor"),
        P("section", None),
        P(None, None, "tensor"),
        P("section", None, "tensor"),
        P("section", None, "tensor"),
        P("section", "tensor", None),
        P("section", None),
    )
    out_specs = (P("section", None, None, "tensor"),) * 3
    return jax.shard_map(on_device, mesh=mesh, in_specs=in_specs, out_specs=out_specs, check_vma=False)
```

time: 805 us -> 136 us (0.17)
  waiting for transfers between devices: 680 us -> 0 us
  Pallas kernels: 0 us -> 128 us
  matrix products: 47.1 us -> 0 us
  other arithmetic: 28.5 us -> 0 us
  starting transfers between devices: 25.4 us -> 0 us
  between operations: 14.5 us -> 0.64 us
    all_gather x5 -> x0, waiting for transfers between devices: 326 us -> none  [the longest x1 75.2 us: on_device(): lax.all_gather(cotangent, 'tensor', axis=2, tiled=True)]
    psum x2 -> x0, waiting for transfers between devices: 316 us -> none  [on_device(): lax.psum(jnp.dot(attended_flat, weight_out, preferred_element_type=jnp.fl...]
    pallas_call x0 -> x1, Pallas kernels: none -> 128 us  [on_device(): pl.pallas_call(kernel, out_shape=(slab, slab, slab), in_specs=[any_spec]...]
    dot_general x22 -> x0, matrix products: 45.3 us -> none  [the longest x4 14.1 us: on_device(): projected = jnp.dot(normed, weight_in, preferred_element_type=jnp.float32)]
    ppermute x10 -> x0, waiting for transfers between devices: 35.7 us -> none  [the longest x8 27.7 us: partner(): return lax.ppermute(value, axis, pairs)]
    ppermute x10 -> x0, starting transfers between devices: 24.9 us -> none  [the longest x8 20.5 us: partner(): return lax.ppermute(value, axis, pairs)]
    reduce_sum x8 -> x0, other arithmetic: 12.6 us -> none  [the longest x3 6.13 us: normalize(): centre = jnp.mean(values, axis=-1, keepdims=True)]
    convert_element_type x3 -> x0, other arithmetic: 8.36 us -> none  [the longest x1 4.37 us: norm_backward(): return (upstream.astype(jnp.float32) + grad_local).astype(jnp.bfloat16)]
  transfers between devices with their start and end apart: 17 -> 0, of which waited for: 16 -> 0; matrix products, arithmetic and copies ran while one was open for 5% -> 0% of each run, Pallas kernels for 0% -> 0%
where the time goes in v1:
time: 136 us; the launch traced here: 135 us
  Pallas kernels  128 us (94%)
  local copies, waits for them, and re-layouts  6.14 us (5%)
    pallas_call x1, Pallas kernels, on_device(): pl.pallas_call(kernel, out_shape=(slab, slab, slab), in_specs=[any_spec]...  128 us
    unnamed x3, local copies, waits for them, and re-layouts  4.7 us

profile of v1, /device:TPU:2, one launch (start us, length us, event | category | flops | bytes accessed | tf_op | source)
XLA Modules:
  0.0 134.9 jit_solution(514654642424868574)
XLA Ops:
  0.6 1.4 %broadcast_in_dim.8.flags = s32[2,128,256]{2,1,0:T(8,128)} broadcast(s32[2]{0:T(128)} %bitcast.1), dimensions={0} | broadcast | bytes 262152 | tf_op jit(solution)/shard_map/broadcast_in_dim | solution.py:445
  2.1 128.1 %relay_window.1 = (bf16[1,2,128,256]{3,2,1,0:T(8,128)(2,1)}, bf16[1,2,128,256]{3,2,1,0:T(8,128)(2,1)}, bf16[1,2,128,256]{3,2,1,0:T(8,128)(2,1)}) custom-call(bf16[2,128,256]{2,1,0:T(8,128)(2,1)} %ent.1, bf16[1,128,256]{2,1,0:T(8,128)(2,1)} %arr.1, bf16[1,2,128,256]{3,2,1,0:T(8,128)(2,1)} %stash.1, bf16[1,2,128,256]{3,2,1,0:T(8,128)(2,1)} %park.1, ...), custom_call_target="tpu_custom_call" | custom-call | flops 6000000000 | bytes 10000000 | tf_op jit(solution)/shard_map/relay_window/pallas_call | solution.py:449
  130.2 1.6 %copy.16 = bf16[1,2,128,256]{3,2,1,0:T(8,128)(2,1)} copy(bf16[1,2,128,256]{3,2,1,0:T(8,128)(2,1)} %get-tuple-element.6) | data formatting | bytes 262144
  131.8 1.6 %copy.17 = bf16[1,2,128,256]{3,2,1,0:T(8,128)(2,1)} copy(bf16[1,2,128,256]{3,2,1,0:T(8,128)(2,1)} %get-tuple-element.7) | data formatting | bytes 262144
  133.3 1.6 %copy.18 = bf16[1,2,128,256]{3,2,1,0:T(8,128)(2,1)} copy(bf16[1,2,128,256]{3,2,1,0:T(8,128)(2,1)} %get-tuple-element.8) | data formatting | bytes 262144

commit v2 on v1

--- a/solution.py
+++ b/solution.py
@@ -31,8 +31,8 @@
 
 def kernel(
     ent, arr, stash, park, flags, cot, agr, wq_h, wo_h, gain_h,
-    out_f, out_b, out_p,
-    wq, wo, gain, stv, prk, flv, ag, normed, proj, att, gab, gpb, wgs,
+    out_all,
+    wq, wo, gain, p1, stv, prk, flv, ag, normed, proj, att, gab, gpb, wgs,
     pbuf, dbuf, zbuf, rrecv, drecv, zrecv, zown, sbuf, srecv, szbuf, szrecv, ostage, pstage,
     lsem, ag_s, agz_r, agy_r, rs_s, rsr_r, rsd_r, rsz_r, st_s, st_r, m_s, m_r, hop_s, hop_r, o_s,
 ):
@@ -277,7 +277,7 @@
     def forward_end(tick):
         total = rs_fin(RF1 if tick else RF0)
         ostage[tick] = (ag[X1 if tick else X0, own].astype(F32) + total).astype(BF)
-        pltpu.make_async_copy(ostage.at[tick], out_f.at[0, tick], o_s.at[tick]).start()
+        pltpu.make_async_copy(ostage.at[tick], out_all.at[0, tick], o_s.at[tick]).start()
 
     def backward_end(tick, mean, inv):
         total = rs_fin(RB1 if tick else RB0)
@@ -285,7 +285,7 @@
         std = (ag[H1 if tick else H0, own].astype(F32) - mean) * inv
         grad = inv * (total * gain[:, my_cols] - m1 - std * m2)
         ostage[2 + tick] = (ag[U1 if tick else U0, own].astype(F32) + grad).astype(BF)
-        pltpu.make_async_copy(ostage.at[2 + tick], out_b.at[0, tick], o_s.at[2 + tick]).start()
+        pltpu.make_async_copy(ostage.at[2 + tick], out_all.at[1, tick], o_s.at[2 + tick]).start()
 
     def hop_start(slot, a, forward):
         cp = rcopy(ostage.at[slot], ag.at[a, own], hop_s.at[slot // 2], hop_r.at[slot // 2], (nxt if forward else prv, t))
@@ -311,17 +311,17 @@
         return rcopy(park.at[0, tick], prk.at[tick], m_s.at[tick], m_r.at[tick], (mir, t))
 
     def parked_copy(tick):
-        return rcopy(pstage.at[tick], out_p.at[0, tick], m_s.at[2 + tick], m_r.at[2 + tick], (mir, t))
+        return rcopy(pstage.at[tick], out_all.at[2, tick], m_s.at[2 + tick], m_r.at[2 + tick], (mir, t))
 
     def park_inflow(tick):
         mine = ag[X1 if tick else X0, own]
-        pstage[tick] = jnp.where(flv[tick] == 1, mine.astype(F32), 0.0).astype(BF)
+        pstage[tick] = jnp.where(flv[:, tick : tick + 1] == 1, mine.astype(F32), 0.0).astype(BF)
         parked_copy(tick).start()
 
     def choose(tick):
         mirror_copy(tick).wait_recv()
         ag[H1 if tick else H0, own] = jnp.where(
-            flv[tick] == 1, prk[tick].astype(F32), stv[tick].astype(F32)
+            flv[:, tick : tick + 1] == 1, prk[tick].astype(F32), stv[tick].astype(F32)
         ).astype(BF)
 
     mirror_copy(0).start()
@@ -329,20 +329,19 @@
     ag_z(X0)
     ag_y1(X0, 0)
     pltpu.make_async_copy(agr.at[0], ag.at[U0, own], lsem.at[1]).wait()
-    mirror_copy(1).start()
     ag_z(U0)
     ag_y1(U0, 0)
     load_stash.wait()
     load_flags.wait()
     load_gain.wait()
-    load_wq.wait()
-    load_wo.wait()
     y1_rest(X0)
-    y1_rest(U0)
-    y2_all(X0)
     choose(0)
     ag_z(H0)
     ag_y1(H0, 0)
+    mirror_copy(1).start()
+    y1_rest(U0)
+    load_wq.wait()
+    load_wo.wait()
     g_hi = gain[...].astype(BF)
     g_lo = (gain[...] - g_hi.astype(F32)).astype(BF)
     sub = lax.broadcasted_iota(jnp.int32, (16, 128), 0)
@@ -356,23 +355,22 @@
         return carry
 
     lax.fori_loop(0, 3, wg_tile, 0)
+    y2_all(X0)
+    y1_rest(H0)
     y2_all(U0)
     choose(1)
-    y1_rest(H0)
     ag_fin(X0)
     layer_norm(X0)
     qkv()
     attended(attention())
+    y2_all(H0)
     rs_o(RF0)
-    y2_all(H0)
-    ag_z(H1)
-    rs_d(RF0)
     ag_fin(U0)
     grad_att(U0)
-    park_inflow(0)
-    rs_z(RF0)
+    rs_d(RF0)
     ag_fin(H0)
     mean0, inv0 = layer_norm(H0)
+    rs_z(RF0)
     qkv()
     heads = attention()
     attend_back(heads)
@@ -380,46 +378,50 @@
     rs_o(RB0)
     forward_end(0)
     hop_start(0, X1, True)
+    ag_z(H1)
+    stats_mid(0)
     rs_d(RB0)
     ag_y1(H1, 0)
-    y1_rest(H1)
-    stats_mid(0)
     hop_wait(0, X1, True, ent.at[1])
     ag_z(X1)
     ag_y1(X1, 0)
+    y1_rest(H1)
     rs_z(RB0)
     y1_rest(X1)
     y2_all(H1)
     backward_end(0, mean0, inv0)
     hop_start(2, U1, False)
     y2_all(X1)
+    park_inflow(0)
     ag_fin(H1)
+    mean1, inv1 = layer_norm(H1)
     hop_wait(2, U1, False, cot.at[1])
     ag_z(U1)
     ag_y1(U1, 0)
+    qkv()
+    heads = attention()
+    p1[...] = proj[...]
+    y1_rest(U1)
     ag_fin(X1)
     layer_norm(X1)
+    y2_all(U1)
     qkv()
     attended(attention())
-    y1_rest(U1)
     rs_o(RF1)
-    y2_all(U1)
-    rs_d(RF1)
-    mean1, inv1 = layer_norm(H1)
-    qkv()
-    heads = attention()
     park_inflow(1)
-    rs_z(RF1)
     ag_fin(U1)
     grad_att(U1)
     attend_back(heads)
+    proj[...] = p1[...]
     stats_start(1)
     rs_o(RB1)
     rs_d(RB1)
+    rs_d(RF1)
     stats_mid(1)
+    rs_z(RB1)
+    rs_z(RF1)
+    backward_end(1, mean1, inv1)
     forward_end(1)
-    rs_z(RB1)
-    backward_end(1, mean1, inv1)
 
     for a in range(6):
         pltpu.make_async_copy(ag.at[a, pl.ds(0, 15)], ag.at[a, pl.ds(0, 15)], ag_s.at[a]).wait()
@@ -428,8 +430,8 @@
     for tick in range(2):
         mirror_copy(tick).wait_send()
         parked_copy(tick).wait()
-        pltpu.make_async_copy(ostage.at[tick], out_f.at[0, tick], o_s.at[tick]).wait()
-        pltpu.make_async_copy(ostage.at[2 + tick], out_b.at[0, tick], o_s.at[2 + tick]).wait()
+        pltpu.make_async_copy(ostage.at[tick], out_all.at[0, tick], o_s.at[tick]).wait()
+        pltpu.make_async_copy(ostage.at[2 + tick], out_all.at[1, tick], o_s.at[2 + tick]).wait()
 
     @pl.when(s < sections - 1)
     def _():
@@ -442,22 +444,22 @@
 
 def on_device(entering, arriving, stashed, parked, evict, cotangent, arriving_grad, qkv_weight, out_weight, norm_gain):
     any_spec = pl.BlockSpec(memory_space=pl.ANY)
-    flags = jnp.broadcast_to(evict[0][:, None, None], (2, 128, 256))
     piece = lambda *lead: pltpu.VMEM(tuple(lead) + (128, 256), BF)
     dma = lambda *shape: pltpu.SemaphoreType.DMA(shape)
-    slab = jax.ShapeDtypeStruct((1, 2, 128, 256), BF)
-    return pl.pallas_call(
+    slab = jax.ShapeDtypeStruct((3, 2, 128, 256), BF)
+    made = pl.pallas_call(
         kernel,
-        out_shape=(slab, slab, slab),
+        out_shape=slab,
         in_specs=[any_spec] * 10,
-        out_specs=(any_spec,) * 3,
+        out_specs=any_spec,
         scratch_shapes=[
             pltpu.VMEM(qkv_weight.shape[1:], BF),
             pltpu.VMEM(out_weight.shape[1:], BF),
             pltpu.VMEM(norm_gain.shape, F32),
+            pltpu.VMEM((128, 768), F32),
             piece(2),
             piece(2),
-            pltpu.VMEM((2, 128, 256), jnp.int32),
+            pltpu.VMEM((1, 2), jnp.int32),
             piece(6, 16),
             pltpu.VMEM((128, 4096), BF),
             pltpu.VMEM((128, 768), F32),
@@ -499,7 +501,9 @@
         ),
         cost_estimate=pl.CostEstimate(flops=6 * 10**9, bytes_accessed=10**7, transcendentals=10**5),
         name="relay_window",
-    )(entering, arriving, stashed, parked, flags, cotangent, arriving_grad, qkv_weight, out_weight, norm_gain)
+    )(entering, arriving, stashed, parked, evict, cotangent, arriving_grad, qkv_weight, out_weight, norm_gain)
+
+    return made[0:1], made[1:2], made[2:3]
 
 
 def solution(mesh):

time: 136 us -> 130 us (0.956)
  local copies, waits for them, and re-layouts: 6.14 us -> 1.78 us
  Pallas kernels: 128 us -> 125 us
    unnamed x3 -> x0, local copies, waits for them, and re-layouts: 4.7 us -> none
    pallas_call x1, Pallas kernels: 128 us -> 125 us  [on_device(): pl.pallas_call(kernel, out_shape=slab, in_specs=[any_spec] * 10, out_spec...]
    slice x0 -> x1, local copies, waits for them, and re-layouts: none -> 1.78 us  [on_device(): return (made[0:1], made[1:2], made[2:3])]
    broadcast_in_dim x1 -> x0, local copies, waits for them, and re-layouts: 1.43 us -> none  [on_device(): flags = jnp.broadcast_to(evict[0][:, None, None], (2, 128, 256))]
where the time goes in v2:
time: 130 us; the launch traced here: 128 us
  Pallas kernels  125 us (96%)
  local copies, waits for them, and re-layouts  1.78 us (1%)
    pallas_call x1, Pallas kernels, on_device(): pl.pallas_call(kernel, out_shape=slab, in_specs=[any_spec] * 10, out_spec...  125 us

profile of v2, /device:TPU:2, one launch (start us, length us, event | category | flops | bytes accessed | tf_op | source)
XLA Modules:
  0.0 127.8 jit_solution(17001250118932204416)
XLA Ops:
  0.6 125.4 %relay_window.1 = bf16[3,2,128,256]{3,2,1,0:T(8,128)(2,1)} custom-call(bf16[2,128,256]{2,1,0:T(8,128)(2,1)} %ent.1, bf16[1,128,256]{2,1,0:T(8,128)(2,1)} %arr.1, bf16[1,2,128,256]{3,2,1,0:T(8,128)(2,1)} %stash.1, bf16[1,2,128,256]{3,2,1,0:T(8,128)(2,1)} %park.1, s32[1,2]{1,0:T(1,128)} %flags.1, bf16[2,128,256]{2,1,0:T(8,128)(2,1)} %cot.1, ...), custom_call_target="tpu_custom_call" | custom-call | flops 6000000000 | bytes 10000000 | tf_op jit(solution)/shard_map/relay_window/pallas_call | solution.py:450
  126.0 1.8 %fusion = (bf16[1,2,128,256]{3,2,1,0:T(8,128)(2,1)}, bf16[1,2,128,256]{3,2,1,0:T(8,128)(2,1)}, bf16[1,2,128,256]{3,2,1,0:T(8,128)(2,1)}) fusion(bf16[3,2,128,256]{3,2,1,0:T(8,128)(2,1)} %relay_window.1), kind=kLoop, calls=%fused_computation | loop fusion | bytes 786432 | tf_op jit(solution)/shard_map/slice | solution.py:506

commit v3 on v2

--- a/solution.py
+++ b/solution.py
@@ -32,9 +32,9 @@
 def kernel(
     ent, arr, stash, park, flags, cot, agr, wq_h, wo_h, gain_h,
     out_all,
-    wq, wo, gain, p1, stv, prk, flv, ag, normed, proj, att, gab, gpb, wgs,
+    wq, wo, gain, p1, gaf, stv, prk, flv, ag, normed, proj, att, gab, gpb, wgs,
     pbuf, dbuf, zbuf, rrecv, drecv, zrecv, zown, sbuf, srecv, szbuf, szrecv, ostage, pstage,
-    lsem, ag_s, agz_r, agy_r, rs_s, rsr_r, rsd_r, rsz_r, st_s, st_r, m_s, m_r, hop_s, hop_r, o_s,
+    lsem, ag_s, agz_r, agy_r, rs_s, rsr_r, rsd_r, rsz_r, st_s, st_r, m_s, m_r, hop_s, hop_r, fz_s, o_s,
 ):
     s, t = lax.axis_index("section"), lax.axis_index("tensor")
     sections = lax.axis_size("section")
@@ -89,7 +89,8 @@
     load_wo.start()
 
     barrier = pltpu.get_barrier_semaphore()
-    peers = [ydev(1), ydev(2), ydev(3), zdev(1), zdev(2), zdev(3), (nxt, t), (prv, t), (mir, t)]
+    peers = [ydev(1), ydev(2), ydev(3), zdev(1), zdev(2), zdev(3), (mir, t)]
+    peers += [(sec, zi[k] * 4 + y) for sec in (nxt, prv) for k in range(4)]
     for dev in peers:
         pl.semaphore_signal(barrier, inc=1, device_id=dev, device_id_type=MESH)
     pl.semaphore_wait(barrier, len(peers))
@@ -185,11 +186,21 @@
         for h, (q, k, v, p, w) in enumerate(heads):
             att[:, h * 128 : (h + 1) * 128] = dot(w, v).astype(BF)
 
-    def grad_att(a):
-        def step(c, acc):
-            return acc + dot_nt(ag[a, c], wo[:, cols(lax.div(c, 4), lax.rem(c, 4))])
-
-        gab[...] = lax.fori_loop(0, 16, step, jnp.zeros((128, 256), F32)).astype(BF)
+    def grad_cols(a, js, first):
+        acc = first
+        for j in js:
+
+            def step(zz, acc, j=j):
+                return acc + dot_nt(ag[a, chunk(yi[j], zz)], wo[:, cols(yi[j], zz)])
+
+            acc = lax.fori_loop(0, 4, step, acc)
+        return acc
+
+    def grad_att3(a):
+        gaf[...] = grad_cols(a, (0, 1, 3), jnp.zeros((128, 256), F32))
+
+    def grad_att1(a):
+        gab[...] = grad_cols(a, (2,), gaf[...]).astype(BF)
 
     def attend_back(heads):
         for h, (q, k, v, p, w) in enumerate(heads):
@@ -241,8 +252,6 @@
         for k in KS:
             pbuf[r, 1, k] = part(r, yi[1], zi[k]).astype(BF)
             pbuf[r, 3, k] = part(r, yi[3], zi[k]).astype(BF)
-        for k in KS:
-            pbuf[r, 0, k] = part(r, y, zi[k]).astype(BF)
 
     def rs_d(r):
         top, low = pl.ds(0, 64), pl.ds(64, 64)
@@ -260,7 +269,7 @@
         for k in KS:
             rcopy(dbuf.at[r, 0, k], drecv.at[r, 0, k], rs_s.at[r], rsd_r.at[r, 0, k], ydev(3)).wait_recv()
             rcopy(dbuf.at[r, 1, k], drecv.at[r, 1, k], rs_s.at[r], rsd_r.at[r, 1, k], ydev(1)).wait_recv()
-            total = pbuf[r, 0, k].astype(F32) + drecv[r, 0, k].astype(F32) + drecv[r, 1, k].astype(F32)
+            total = part(r, y, zi[k]).astype(BF).astype(F32) + drecv[r, 0, k].astype(F32) + drecv[r, 1, k].astype(F32)
             if k:
                 zbuf[r, k - 1] = total.astype(BF)
                 rcopy(zbuf.at[r, k - 1], zrecv.at[r, k - 1], rs_s.at[r], rsz_r.at[r, k - 1], zdev(k)).start()
@@ -287,15 +296,22 @@
         ostage[2 + tick] = (ag[U1 if tick else U0, own].astype(F32) + grad).astype(BF)
         pltpu.make_async_copy(ostage.at[2 + tick], out_all.at[1, tick], o_s.at[2 + tick]).start()
 
+    def hop_copy(slot, a, forward, k):
+        to = nxt if forward else prv
+        recv = agz_r.at[a, k - 1] if k else hop_r.at[slot // 2]
+        return rcopy(ostage.at[slot], ag.at[a, own], hop_s.at[slot // 2, k], recv, (to, zi[k] * 4 + y))
+
     def hop_start(slot, a, forward):
-        cp = rcopy(ostage.at[slot], ag.at[a, own], hop_s.at[slot // 2], hop_r.at[slot // 2], (nxt if forward else prv, t))
-
         @pl.when((s < sections - 1) if forward else (s > 0))
         def _():
-            cp.start()
+            for k in (0, 1, 3, 2):
+                hop_copy(slot, a, forward, k).start()
+
+    def first_z(slot, a, k):
+        return rcopy(ag.at[a, own], ag.at[a, own], fz_s.at[slot // 2, k - 1], agz_r.at[a, k - 1], zdev(k))
 
     def hop_wait(slot, a, forward, first):
-        cp = rcopy(ostage.at[slot], ag.at[a, own], hop_s.at[slot // 2], hop_r.at[slot // 2], (prv if forward else nxt, t))
+        cp = rcopy(ostage.at[slot], ag.at[a, own], hop_s.at[slot // 2, 0], hop_r.at[slot // 2], (prv if forward else nxt, t))
 
         @pl.when((s > 0) if forward else (s < sections - 1))
         def _():
@@ -306,6 +322,8 @@
             own_copy = pltpu.make_async_copy(first, ag.at[a, own], lsem.at[slot // 2])
             own_copy.start()
             own_copy.wait()
+            for k in (1, 3, 2):
+                first_z(slot, a, k).start()
 
     def mirror_copy(tick):
         return rcopy(park.at[0, tick], prk.at[tick], m_s.at[tick], m_r.at[tick], (mir, t))
@@ -329,17 +347,15 @@
     ag_z(X0)
     ag_y1(X0, 0)
     pltpu.make_async_copy(agr.at[0], ag.at[U0, own], lsem.at[1]).wait()
-    ag_z(U0)
     ag_y1(U0, 0)
     load_stash.wait()
     load_flags.wait()
     load_gain.wait()
     y1_rest(X0)
+    ag_z(U0)
     choose(0)
     ag_z(H0)
     ag_y1(H0, 0)
-    mirror_copy(1).start()
-    y1_rest(U0)
     load_wq.wait()
     load_wo.wait()
     g_hi = gain[...].astype(BF)
@@ -356,23 +372,26 @@
 
     lax.fori_loop(0, 3, wg_tile, 0)
     y2_all(X0)
+    y1_rest(U0)
+    mirror_copy(1).start()
     y1_rest(H0)
     y2_all(U0)
-    choose(1)
     ag_fin(X0)
     layer_norm(X0)
     qkv()
     attended(attention())
     y2_all(H0)
     rs_o(RF0)
+    grad_att3(U0)
     ag_fin(U0)
-    grad_att(U0)
+    grad_att1(U0)
     rs_d(RF0)
     ag_fin(H0)
     mean0, inv0 = layer_norm(H0)
     rs_z(RF0)
     qkv()
     heads = attention()
+    choose(1)
     attend_back(heads)
     stats_start(0)
     rs_o(RB0)
@@ -383,7 +402,6 @@
     rs_d(RB0)
     ag_y1(H1, 0)
     hop_wait(0, X1, True, ent.at[1])
-    ag_z(X1)
     ag_y1(X1, 0)
     y1_rest(H1)
     rs_z(RB0)
@@ -396,7 +414,6 @@
     ag_fin(H1)
     mean1, inv1 = layer_norm(H1)
     hop_wait(2, U1, False, cot.at[1])
-    ag_z(U1)
     ag_y1(U1, 0)
     qkv()
     heads = attention()
@@ -409,22 +426,24 @@
     attended(attention())
     rs_o(RF1)
     park_inflow(1)
+    grad_att3(U1)
+    rs_d(RF1)
     ag_fin(U1)
-    grad_att(U1)
+    grad_att1(U1)
     attend_back(heads)
     proj[...] = p1[...]
     stats_start(1)
     rs_o(RB1)
+    rs_z(RF1)
     rs_d(RB1)
-    rs_d(RF1)
     stats_mid(1)
+    forward_end(1)
     rs_z(RB1)
-    rs_z(RF1)
     backward_end(1, mean1, inv1)
-    forward_end(1)
 
     for a in range(6):
-        pltpu.make_async_copy(ag.at[a, pl.ds(0, 15)], ag.at[a, pl.ds(0, 15)], ag_s.at[a]).wait()
+        sent = pl.ds(0, 12 if a in (X1, U1) else 15)
+        pltpu.make_async_copy(ag.at[a, sent], ag.at[a, sent], ag_s.at[a]).wait()
     for r in range(4):
         pltpu.make_async_copy(ag.at[0, pl.ds(0, 15)], ag.at[0, pl.ds(0, 15)], rs_s.at[r]).wait()
     for tick in range(2):
@@ -433,13 +452,17 @@
         pltpu.make_async_copy(ostage.at[tick], out_all.at[0, tick], o_s.at[tick]).wait()
         pltpu.make_async_copy(ostage.at[2 + tick], out_all.at[1, tick], o_s.at[2 + tick]).wait()
 
-    @pl.when(s < sections - 1)
-    def _():
-        rcopy(ostage.at[0], ag.at[X1, own], hop_s.at[0], hop_r.at[0], (nxt, t)).wait_send()
-
-    @pl.when(s > 0)
-    def _():
-        rcopy(ostage.at[2], ag.at[U1, own], hop_s.at[1], hop_r.at[1], (prv, t)).wait_send()
+    for slot, a, forward in ((0, X1, True), (2, U1, False)):
+
+        @pl.when((s < sections - 1) if forward else (s > 0))
+        def _():
+            for k in range(4):
+                hop_copy(slot, a, forward, k).wait_send()
+
+        @pl.when((s == 0) if forward else (s == sections - 1))
+        def _():
+            for k in (1, 2, 3):
+                first_z(slot, a, k).wait_send()
 
 
 def on_device(entering, arriving, stashed, parked, evict, cotangent, arriving_grad, qkv_weight, out_weight, norm_gain):
@@ -457,6 +480,7 @@
             pltpu.VMEM(out_weight.shape[1:], BF),
             pltpu.VMEM(norm_gain.shape, F32),
             pltpu.VMEM((128, 768), F32),
+            pltpu.VMEM((128, 256), F32),
             piece(2),
             piece(2),
             pltpu.VMEM((1, 2), jnp.int32),
@@ -492,8 +516,9 @@
             dma(2, 6),
             dma(4),
             dma(4),
+            dma(2, 4),
             dma(2),
-            dma(2),
+            dma(2, 3),
             dma(4),
         ],
         compiler_params=pltpu.CompilerParams(

time: 130 us -> 124 us (0.954); the launches traced: 128 us -> 124 us
  Pallas kernels: 125 us -> 122 us
    pallas_call x1, Pallas kernels: 125 us -> 122 us  [on_device(): pl.pallas_call(kernel, out_shape=slab, in_specs=[any_spec] * 10, out_spec...]
where the time goes in v3:
time: 124 us
  Pallas kernels  122 us (98%)
  local copies, waits for them, and re-layouts  1.78 us (1%)
    pallas_call x1, Pallas kernels, on_device(): pl.pallas_call(kernel, out_shape=slab, in_specs=[any_spec] * 10, out_spec...  122 us

profile of v3, /device:TPU:2, one launch (start us, length us, event | category | flops | bytes accessed | tf_op | source)
XLA Modules:
  0.0 124.0 jit_solution(3018722252450547347)
XLA Ops:
  0.6 121.6 %relay_window.1 = bf16[3,2,128,256]{3,2,1,0:T(8,128)(2,1)} custom-call(bf16[2,128,256]{2,1,0:T(8,128)(2,1)} %ent.1, bf16[1,128,256]{2,1,0:T(8,128)(2,1)} %arr.1, bf16[1,2,128,256]{3,2,1,0:T(8,128)(2,1)} %stash.1, bf16[1,2,128,256]{3,2,1,0:T(8,128)(2,1)} %park.1, s32[1,2]{1,0:T(1,128)} %flags.1, bf16[2,128,256]{2,1,0:T(8,128)(2,1)} %cot.1, ...), custom_call_target="tpu_custom_call" | custom-call | flops 6000000000 | bytes 10000000 | tf_op jit(solution)/shard_map/relay_window/pallas_call | solution.py:473
  122.3 1.8 %fusion = (bf16[1,2,128,256]{3,2,1,0:T(8,128)(2,1)}, bf16[1,2,128,256]{3,2,1,0:T(8,128)(2,1)}, bf16[1,2,128,256]{3,2,1,0:T(8,128)(2,1)}) fusion(bf16[3,2,128,256]{3,2,1,0:T(8,128)(2,1)} %relay_window.1), kind=kLoop, calls=%fused_computation | loop fusion | bytes 786432 | tf_op jit(solution)/shard_map/slice | solution.py:531

commit v4 on v3

--- a/solution.py
+++ b/solution.py
@@ -143,14 +143,14 @@
         def add(c, acc):
             return acc + ag[a, c].astype(F32)
 
-        acc = lax.fori_loop(0, 16, add, jnp.zeros((128, 256), F32))
+        acc = lax.fori_loop(0, 16, add, jnp.zeros((128, 256), F32), unroll=4)
         mean = jnp.sum(acc, axis=1, keepdims=True) * (1.0 / feats)
 
         def var(c, acc):
             d = ag[a, c].astype(F32) - mean
             return acc + d * d
 
-        acc = lax.fori_loop(0, 16, var, jnp.zeros((128, 256), F32))
+        acc = lax.fori_loop(0, 16, var, jnp.zeros((128, 256), F32), unroll=4)
         inv = lax.rsqrt(jnp.sum(acc, axis=1, keepdims=True) * (1.0 / feats) + 1e-05)
 
         def put(c, carry):
@@ -158,7 +158,7 @@
             normed[:, cc] = ((ag[a, c].astype(F32) - mean) * inv * gain[:, cc]).astype(BF)
             return carry
 
-        lax.fori_loop(0, 16, put, 0)
+        lax.fori_loop(0, 16, put, 0, unroll=4)
         return mean, inv
 
     def qkv():
@@ -167,7 +167,7 @@
             proj[:, nn] = dot(normed[...], wq[:, nn])
             return carry
 
-        lax.fori_loop(0, 3, tile, 0)
+        lax.fori_loop(0, 3, tile, 0, unroll=3)
 
     scale = 1.0 / math.sqrt(HD)
 
@@ -193,7 +193,7 @@
             def step(zz, acc, j=j):
                 return acc + dot_nt(ag[a, chunk(yi[j], zz)], wo[:, cols(yi[j], zz)])
 
-            acc = lax.fori_loop(0, 4, step, acc)
+            acc = lax.fori_loop(0, 4, step, acc, unroll=4)
         return acc
 
     def grad_att3(a):

time: 124 us -> 123 us (level)
  no operation moved by 1% of the time
where the time goes in v4:
time: 123 us
  Pallas kernels  121 us (98%)
  local copies, waits for them, and re-layouts  1.78 us (1%)
    pallas_call x1, Pallas kernels, on_device(): pl.pallas_call(kernel, out_shape=slab, in_specs=[any_spec] * 10, out_spec...  121 us

profile of v4, /device:TPU:2, one launch (start us, length us, event | category | flops | bytes accessed | tf_op | source)
XLA Modules:
  0.0 122.9 jit_solution(12824613049159598092)
XLA Ops:
  0.6 120.5 %relay_window.1 = bf16[3,2,128,256]{3,2,1,0:T(8,128)(2,1)} custom-call(bf16[2,128,256]{2,1,0:T(8,128)(2,1)} %ent.1, bf16[1,128,256]{2,1,0:T(8,128)(2,1)} %arr.1, bf16[1,2,128,256]{3,2,1,0:T(8,128)(2,1)} %stash.1, bf16[1,2,128,256]{3,2,1,0:T(8,128)(2,1)} %park.1, s32[1,2]{1,0:T(1,128)} %flags.1, bf16[2,128,256]{2,1,0:T(8,128)(2,1)} %cot.1, ...), custom_call_target="tpu_custom_call" | custom-call | flops 6000000000 | bytes 10000000 | tf_op jit(solution)/shard_map/relay_window/pallas_call | solution.py:473
  121.1 1.8 %fusion = (bf16[1,2,128,256]{3,2,1,0:T(8,128)(2,1)}, bf16[1,2,128,256]{3,2,1,0:T(8,128)(2,1)}, bf16[1,2,128,256]{3,2,1,0:T(8,128)(2,1)}) fusion(bf16[3,2,128,256]{3,2,1,0:T(8,128)(2,1)} %relay_window.1), kind=kLoop, calls=%fused_computation | loop fusion | bytes 786432 | tf_op jit(solution)/shard_map/slice | solution.py:531
